TPU v7x, 512 devices: a whole 4x4x16 slice. The times are simulated.
512 devices in a mesh: row: 16 (over x, y), col: 16 (over z_lo, core), ch: 2 (over z_hi).
Axes of the slice: x: 4, y: 4, z: 16 (z_hi: 2, z_lo: 8; z = z_hi * 8 + z_lo), core: 2. Of those that a mesh axis runs over, the one named last changes fastest.
Arguments:
- image: bfloat16 [512, 512, 512], P('row', 'col', 'ch'), may hold values from -6 to 6
- weight_one: bfloat16 [3, 3, 512, 512], P(None, None, None, 'ch'), may hold values from -0.09375 to 0.09375
- scale_one: float32 [512], P('ch'), may hold values from 0.1 to 1.9
- shift_one: float32 [512], P('ch'), may hold values from -0.5 to 0.5
- weight_two: bfloat16 [3, 3, 512, 512], P(None, None, None, 'ch'), may hold values from -0.09375 to 0.09375
- scale_two: float32 [512], P('ch'), may hold values from 0.1 to 1.9
- shift_two: float32 [512], P('ch'), may hold values from -0.5 to 0.5
Outputs:
- features: bfloat16 [512, 512, 512], P('row', 'col', 'ch')
All inputs are finite; a program needn't handle non-finite values.
Results may differ from a plain program's by a relative error of at most 0.0048.
Values may be sent and summed in bfloat16 or wider, within the bound.
A program may use at most 64 MiB of HBM per device.

v0:
```python
import jax
import jax.numpy as jnp
from jax import lax
from jax.sharding import PartitionSpec as P


def with_halo(cells, sides, width):
    for axis, dim in sides:
        count = lax.axis_size(axis)
        ends = count - 1
        head = lax.slice_in_dim(cells, 0, width, axis=dim)
        tail = lax.slice_in_dim(cells, cells.shape[dim] - width, cells.shape[dim], axis=dim)
        cells = jnp.concatenate(
            [
                lax.ppermute(tail, axis, [(i, (i + 1) % count) for i in range(ends)]),
                cells,
                lax.ppermute(head, axis, [((i + 1) % count, i) for i in range(ends)]),
            ],
            axis=dim,
        )
    return cells


def convolve(padded, weight):
    result = lax.conv_general_dilated(
        padded[None],
        weight,
        (1, 1),
        "VALID",
        dimension_numbers=("NHWC", "HWIO", "NHWC"),
        preferred_element_type=jnp.float32,
    )
    return result[0]


def activate(conv_sum, scale, shift):
    return jnp.maximum(conv_sum * scale + shift, 0.0)


def layer_input(source, depth_cells):
    whole = lax.all_gather(source, "ch", axis=2, tiled=True)
    return with_halo(whole, (("row", 0), ("col", 1)), depth_cells)


def shards(image, weight_one, scale_one, shift_one, weight_two, scale_two, shift_two):
    padded = layer_input(image, 1)
    hidden = activate(convolve(padded, weight_one), scale_one, shift_one).astype(jnp.bfloat16)
    second_input = layer_input(hidden, 1)
    return activate(convolve(second_input, weight_two), scale_two, shift_two).astype(jnp.bfloat16)


def solution(mesh):
    return jax.shard_map(
        shards,
        mesh=mesh,
        in_specs=(
            P("row", "col", "ch"),
            P(None, None, None, "ch"),
            P("ch"),
            P("ch"),
            P(None, None, None, "ch"),
            P("ch"),
            P("ch"),
        ),
        out_specs=P("row", "col", "ch"),
        check_vma=False,
    )
```

profile of v0, /device:TPU:89, one launch (start us, length us, event | category | flops | bytes accessed | tf_op | source)
XLA Modules:
  0.0 216.5 jit_solution(8262709917325078321)
XLA Ops:
  6.5 0.7 all-gather.3.cloned.1.call-update
  7.3 70.7 %all-gather.3.cloned.1.call-done = bf16[32,32,512]{2,1,0:T(8,128)(2,1)} async-done(((bf16[32,32,256]{2,1,0:T(8,128)(2,1)}), bf16[32,32,512]{2,1,0:T(8,128)(2,1)}) %all-gather.3.cloned.1.call-update) | async-done | bytes 1048592 | tf_op jit(solution)/shard_map/all_gather | solution.py:41
  78.0 0.8 fusion.40
  78.8 3.0 %collective-permute-start = (bf16[1,32,512]{2,1,0:T(8,128)(2,1)S(1)}, bf16[1,32,512]{2,1,0:T(8,128)(2,1)S(1)}, u32[]{:S(2)}, u32[]{:S(2)}) collective-permute-start(bf16[1,32,512]{2,1,0:T(8,128)(2,1)S(1)} %get-tuple-element.12), channel_id=1, source_target_pairs={{0,32},{32,64},{64,96},{96,128},{128,160},{160,192},{192,224},{224... | collective-permute-start | bytes 98312 | tf_op jit(solution)/shard_map/ppermute | solution.py:15
  81.8 2.3 %collective-permute-start.1 = (bf16[1,32,512]{2,1,0:T(8,128)(2,1)S(1)}, bf16[1,32,512]{2,1,0:T(8,128)(2,1)S(1)}, u32[]{:S(2)}, u32[]{:S(2)}) collective-permute-start(bf16[1,32,512]{2,1,0:T(8,128)(2,1)S(1)} %get-tuple-element.11), channel_id=1, source_target_pairs={{32,0},{64,32},{96,64},{128,96},{160,128},{192,160},{224,192},{256... | collective-permute-start | bytes 98312 | tf_op jit(solution)/shard_map/ppermute | solution.py:17
  84.1 1.3 constant_dynamic-update-slice_fusion.1
  85.4 3.2 %collective-permute-done.1 = bf16[1,32,512]{2,1,0:T(8,128)(2,1)S(1)} collective-permute-done((bf16[1,32,512]{2,1,0:T(8,128)(2,1)S(1)}, bf16[1,32,512]{2,1,0:T(8,128)(2,1)S(1)}, u32[]{:S(2)}, u32[]{:S(2)}) %collective-permute-start.1) | collective-permute-done | bytes 32800 | tf_op jit(solution)/shard_map/ppermute | solution.py:17
  88.7 12.9 %collective-permute-start.2 = (bf16[34,1,512]{2,1,0:T(2,128)(2,1)S(1)}, bf16[34,1,512]{2,1,0:T(2,128)(2,1)S(1)}, u32[]{:S(2)}, u32[]{:S(2)}) collective-permute-start(bf16[34,1,512]{2,1,0:T(2,128)(2,1)S(1)} %get-tuple-element.7), channel_id=1, source_target_pairs={{0,2},{2,4},{4,6},{6,8},{8,10},{10,12},{12,14},{14,16},{16,18},{18... | collective-permute-start | bytes 104456 | tf_op jit(solution)/shard_map/ppermute | solution.py:15
  101.5 1.9 collective-permute-start.3
  103.5 3.7 %collective-permute-done.3 = bf16[34,1,512]{2,1,0:T(2,128)(2,1)S(1)} collective-permute-done((bf16[34,1,512]{2,1,0:T(2,128)(2,1)S(1)}, bf16[34,1,512]{2,1,0:T(2,128)(2,1)S(1)}, u32[]{:S(2)}, u32[]{:S(2)}) %collective-permute-start.3) | collective-permute-done | bytes 34848 | tf_op jit(solution)/shard_map/ppermute | solution.py:17
  107.2 0.8 maximum_bitcast_fusion
  108.0 0.4 copy.16
  108.5 0.4 copy.10
  109.2 3.4 %fusion.19 = f32[32,8,5,256]{3,1,2,0:T(8,128)S(1)} fusion(bf16[3,3,512,256]{3,2,1,0:T(8,128)(2,1)S(1)} %copy-done, bf16[34,1,7,2,512]{4,2,3,0,1:T(8,128)(2,1)S(1)} %slice.40, bf16[34,1,8,5,512]{4,2,3,0,1:T(8,128)(2,1)S(1)} %copy.10, pred[8,5]{0,1:T(8,128)(4,1)S(1)} %copy-done.7), kind=kOutput, calls=%fused_computation.18 | convolution fusion | flops 3026075648 | bytes 5550120 | tf_op jit(solution)/shard_map/conv_general_dilated | solution.py:25
  112.6 0.4 copy.11
  113.1 0.2 copy-done.2
  113.3 0.9 fusion.29
  114.3 57.1 %all-gather.5.cloned.1.call-done = bf16[32,32,512]{2,0,1:T(8,128)(2,1)} async-done(((bf16[32,32,256]{2,0,1:T(8,128)(2,1)}), bf16[32,32,512]{2,0,1:T(8,128)(2,1)}) %all-gather.5.cloned.1.call-update) | async-done | bytes 1048592 | tf_op jit(solution)/shard_map/all_gather | solution.py:41
  171.3 1.2 fusion.39
  172.6 3.0 %collective-permute-start.4 = (bf16[1,32,512]{2,0,1:T(2,128)(2,1)S(1)}, bf16[1,32,512]{2,0,1:T(2,128)(2,1)S(1)}, u32[]{:S(2)}, u32[]{:S(2)}) collective-permute-start(bf16[1,32,512]{2,0,1:T(2,128)(2,1)S(1)} %get-tuple-element.9), channel_id=1, source_target_pairs={{0,32},{32,64},{64,96},{96,128},{128,160},{160,192},{192,224},{224... | collective-permute-start | bytes 98312 | tf_op jit(solution)/shard_map/ppermute | solution.py:15
  175.6 2.2 %collective-permute-start.5 = (bf16[1,32,512]{2,0,1:T(2,128)(2,1)S(1)}, bf16[1,32,512]{2,0,1:T(2,128)(2,1)S(1)}, u32[]{:S(2)}, u32[]{:S(2)}) collective-permute-start(bf16[1,32,512]{2,0,1:T(2,128)(2,1)S(1)} %get-tuple-element.10), channel_id=1, source_target_pairs={{32,0},{64,32},{96,64},{128,96},{160,128},{192,160},{224,192},{256... | collective-permute-start | bytes 98312 | tf_op jit(solution)/shard_map/ppermute | solution.py:17
  177.9 4.9 %collective-permute-done.5 = bf16[1,32,512]{2,0,1:T(2,128)(2,1)S(1)} collective-permute-done((bf16[1,32,512]{2,0,1:T(2,128)(2,1)S(1)}, bf16[1,32,512]{2,0,1:T(2,128)(2,1)S(1)}, u32[]{:S(2)}, u32[]{:S(2)}) %collective-permute-start.5) | collective-permute-done | bytes 32800 | tf_op jit(solution)/shard_map/ppermute | solution.py:17
  182.7 0.8 pad_maximum_fusion.2
  183.5 12.9 %collective-permute-start.6 = (bf16[34,1,512]{2,0,1:T(8,128)(2,1)S(1)}, bf16[34,1,512]{2,0,1:T(8,128)(2,1)S(1)}, u32[]{:S(2)}, u32[]{:S(2)}) collective-permute-start(bf16[34,1,512]{2,0,1:T(8,128)(2,1)S(1)} %get-tuple-element.5), channel_id=1, source_target_pairs={{0,2},{2,4},{4,6},{6,8},{8,10},{10,12},{12,14},{14,16},{16,18},{18... | collective-permute-start | bytes 104456 | tf_op jit(solution)/shard_map/ppermute | solution.py:15
  196.4 1.9 collective-permute-start.7
  198.3 3.4 %collective-permute-done.7 = bf16[34,1,512]{2,0,1:T(8,128)(2,1)S(1)} collective-permute-done((bf16[34,1,512]{2,0,1:T(8,128)(2,1)S(1)}, bf16[34,1,512]{2,0,1:T(8,128)(2,1)S(1)}, u32[]{:S(2)}, u32[]{:S(2)}) %collective-permute-start.7) | collective-permute-done | bytes 34848 | tf_op jit(solution)/shard_map/ppermute | solution.py:17
  201.7 0.8 maximum_bitcast_fusion.1
  202.6 0.4 copy.13
  203.2 1.1 copy-done.6
  204.3 3.4 %fusion.16 = f32[32,8,5,256]{3,1,2,0:T(8,128)S(1)} fusion(bf16[3,3,512,256]{3,2,1,0:T(8,128)(2,1)S(1)} %copy-done.6, bf16[34,1,7,2,512]{4,2,3,0,1:T(8,128)(2,1)S(1)} %slice.44, bf16[34,1,8,5,512]{4,2,3,0,1:T(8,128)(2,1)S(1)} %copy.13, pred[8,5]{0,1:T(8,128)(4,1)S(1)} %copy-done.7), kind=kOutput, calls=%fused_computation.17 | convolution fusion | flops 3026075648 | bytes 5550120 | tf_op jit(solution)/shard_map/conv_general_dilated | solution.py:25
  207.8 0.4 copy.14
  208.6 1.1 copy.15
  (29 shorter events, 1.2 us)
Async XLA Ops:
  6.5 102.6 %copy-start = (bf16[3,3,512,256]{3,2,1,0:T(8,128)(2,1)S(1)}, bf16[3,3,512,256]{3,2,1,0:T(8,128)(2,1)}, u32[]{:S(2)}) copy-start(bf16[3,3,512,256]{3,2,1,0:T(8,128)(2,1)} %param.8) | copy-start | bytes 7077892
  6.5 71.4 %all-gather.3.cloned.1.call-start = ((), (), s32[]{:S(2)}) async-start(), calls=%async_computation | async-start | bytes 1572864 | tf_op jit(solution)/shard_map/all_gather | solution.py:41
  7.3 164.1 %all-gather.5.cloned.1.call-start = ((), (), s32[]{:S(2)}) async-start(), calls=%async_computation.1 | async-start | bytes 1572864 | tf_op jit(solution)/shard_map/all_gather | solution.py:41
  78.8 5.3 %collective-permute-start = (bf16[1,32,512]{2,1,0:T(8,128)(2,1)S(1)}, bf16[1,32,512]{2,1,0:T(8,128)(2,1)S(1)}, u32[]{:S(2)}, u32[]{:S(2)}) collective-permute-start(bf16[1,32,512]{2,1,0:T(8,128)(2,1)S(1)} %get-tuple-element.12), channel_id=1, source_target_pairs={{0,32},{32,64},{64,96},{96,128},{128,160},{160,192},{192,224},{224... | collective-permute-start | bytes 98312 | tf_op jit(solution)/shard_map/ppermute | solution.py:15
  81.8 6.8 %collective-permute-start.1 = (bf16[1,32,512]{2,1,0:T(8,128)(2,1)S(1)}, bf16[1,32,512]{2,1,0:T(8,128)(2,1)S(1)}, u32[]{:S(2)}, u32[]{:S(2)}) collective-permute-start(bf16[1,32,512]{2,1,0:T(8,128)(2,1)S(1)} %get-tuple-element.11), channel_id=1, source_target_pairs={{32,0},{64,32},{96,64},{128,96},{160,128},{192,160},{224,192},{256... | collective-permute-start | bytes 98312 | tf_op jit(solution)/shard_map/ppermute | solution.py:17
  88.7 14.8 %collective-permute-start.2 = (bf16[34,1,512]{2,1,0:T(2,128)(2,1)S(1)}, bf16[34,1,512]{2,1,0:T(2,128)(2,1)S(1)}, u32[]{:S(2)}, u32[]{:S(2)}) collective-permute-start(bf16[34,1,512]{2,1,0:T(2,128)(2,1)S(1)} %get-tuple-element.7), channel_id=1, source_target_pairs={{0,2},{2,4},{4,6},{6,8},{8,10},{10,12},{12,14},{14,16},{16,18},{18... | collective-permute-start | bytes 104456 | tf_op jit(solution)/shard_map/ppermute | solution.py:15
  101.5 5.6 %collective-permute-start.3 = (bf16[34,1,512]{2,1,0:T(2,128)(2,1)S(1)}, bf16[34,1,512]{2,1,0:T(2,128)(2,1)S(1)}, u32[]{:S(2)}, u32[]{:S(2)}) collective-permute-start(bf16[34,1,512]{2,1,0:T(2,128)(2,1)S(1)} %get-tuple-element.8), channel_id=1, source_target_pairs={{2,0},{4,2},{6,4},{8,6},{10,8},{12,10},{14,12},{16,14},{18,16},{20... | collective-permute-start | bytes 104456 | tf_op jit(solution)/shard_map/ppermute | solution.py:17
  108.5 0.7 copy-start.7
  112.6 0.7 copy-start.2
  112.6 0.7 copy-start.3
  171.3 30.4 %copy-start.1 = (bf16[32,32,512]{2,0,1:T(8,128)(2,1)S(1)}, bf16[32,32,512]{2,0,1:T(8,128)(2,1)}, u32[]{:S(2)}) copy-start(bf16[32,32,512]{2,0,1:T(8,128)(2,1)} %all-gather.5.cloned.1.call-done) | copy-start | bytes 3145732
  172.6 5.3 %collective-permute-start.4 = (bf16[1,32,512]{2,0,1:T(2,128)(2,1)S(1)}, bf16[1,32,512]{2,0,1:T(2,128)(2,1)S(1)}, u32[]{:S(2)}, u32[]{:S(2)}) collective-permute-start(bf16[1,32,512]{2,0,1:T(2,128)(2,1)S(1)} %get-tuple-element.9), channel_id=1, source_target_pairs={{0,32},{32,64},{64,96},{96,128},{128,160},{160,192},{192,224},{224... | collective-permute-start | bytes 98312 | tf_op jit(solution)/shard_map/ppermute | solution.py:15
  175.6 7.1 %collective-permute-start.5 = (bf16[1,32,512]{2,0,1:T(2,128)(2,1)S(1)}, bf16[1,32,512]{2,0,1:T(2,128)(2,1)S(1)}, u32[]{:S(2)}, u32[]{:S(2)}) collective-permute-start(bf16[1,32,512]{2,0,1:T(2,128)(2,1)S(1)} %get-tuple-element.10), channel_id=1, source_target_pairs={{32,0},{64,32},{96,64},{128,96},{160,128},{192,160},{224,192},{256... | collective-permute-start | bytes 98312 | tf_op jit(solution)/shard_map/ppermute | solution.py:17
  183.5 14.8 %collective-permute-start.6 = (bf16[34,1,512]{2,0,1:T(8,128)(2,1)S(1)}, bf16[34,1,512]{2,0,1:T(8,128)(2,1)S(1)}, u32[]{:S(2)}, u32[]{:S(2)}) collective-permute-start(bf16[34,1,512]{2,0,1:T(8,128)(2,1)S(1)} %get-tuple-element.5), channel_id=1, source_target_pairs={{0,2},{2,4},{4,6},{6,8},{8,10},{10,12},{12,14},{14,16},{16,18},{18... | collective-permute-start | bytes 104456 | tf_op jit(solution)/shard_map/ppermute | solution.py:15
  196.4 5.3 %collective-permute-start.7 = (bf16[34,1,512]{2,0,1:T(8,128)(2,1)S(1)}, bf16[34,1,512]{2,0,1:T(8,128)(2,1)S(1)}, u32[]{:S(2)}, u32[]{:S(2)}) collective-permute-start(bf16[34,1,512]{2,0,1:T(8,128)(2,1)S(1)} %get-tuple-element.6), channel_id=1, source_target_pairs={{2,0},{4,2},{6,4},{8,6},{10,8},{12,10},{14,12},{16,14},{18,16},{20... | collective-permute-start | bytes 104456 | tf_op jit(solution)/shard_map/ppermute | solution.py:17
  202.6 1.7 copy-start.6
  207.7 0.7 copy-start.4
  207.7 0.7 copy-start.5
Sparse Core Ops, SparseCore 0:
  9.4 68.4 all-gather.2
  114.4 56.8 all-gather.4
where the time goes:
time: 217 us
  waiting for transfers between devices  144 us (66%)
  starting transfers between devices  40.2 us (19%)
  between operations  13.7 us (6%)
  local copies, waits for them, and re-layouts  8.8 us (4%)
  matrix products  6.85 us (3%)
  other arithmetic  3.46 us (2%)
    all_gather x2, waiting for transfers between devices, layer_input(): whole = lax.all_gather(source, 'ch', axis=2, tiled=True)  128 us
    ppermute x4, starting transfers between devices, with_halo(): lax.ppermute(tail, axis, [(i, (i + 1) % count) for i in range(ends)])  31.8 us
    ppermute x4, waiting for transfers between devices, with_halo(): lax.ppermute(head, axis, [((i + 1) % count, i) for i in range(ends)])  15.1 us
    ppermute x4, starting transfers between devices, with_halo(): lax.ppermute(head, axis, [((i + 1) % count, i) for i in range(ends)])  8.35 us
    conv_general_dilated x2, matrix products, convolve(): lax.conv_general_dilated(padded[None], weight, (1, 1), 'VALID', dimension...  6.85 us
  transfers between devices with their start and end apart: 10, of which 6 were waited for; matrix products, arithmetic and copies ran while one was open for 1% of the time, Pallas kernels for 0%

commit v1 on v0

v1 whole, which is shorter than its diff:
```python
import jax
import jax.numpy as jnp
from jax import lax
from jax.experimental import pallas as pl
from jax.experimental.pallas import tpu as pltpu
from jax.sharding import PartitionSpec as P

MESH = pl.DeviceIdType.MESH
F32 = jnp.float32
BF16 = jnp.bfloat16
TILE = 32
HALF = 256
EXT = TILE + 4
HID = TILE + 2
TAPS = 9 * 2 * HALF

CHUNKS = ((0, 8), (24, 8), (8, 8), (16, 4), (20, 4))
OWN_TOP, OWN_BOTTOM, TOP, BOTTOM = 0, 1, 2, 3
GROUPS = ((0, 2), (34, 2), (0, 2), (34, 2)) + tuple((r + 2, n) for r, n in CHUNKS)
CHUNK_SLOT = 4


class Sems:
    def __init__(self, send, recv):
        self.send, self.recv, self.used = send, recv, 0

    def copy(self, src, dst, device):
        i = self.used
        self.used += 1
        return pltpu.make_async_remote_copy(
            src, dst, self.send.at[i], self.recv.at[i], device_id=device, device_id_type=MESH
        )


N_SEMS = 48


def kernel(
    rows, cols,
    img, w1_own, s1, t1, w2_own, s2, t2,
    out,
    x, hid, w1, w2, strip, edge, msg_out, msg_in, big_out, big_in, acc, result, s1all, t1all,
    send_sem, recv_sem, local_sem, out_sem,
):
    r, c, h = lax.axis_index("row"), lax.axis_index("col"), lax.axis_index("ch")
    o = 1 - h
    side = int(round(rows**0.5))
    levels = cols // 2
    px, py = r // side, r % side
    zl, core = c // 2, c % 2
    sems = Sems(send_sem, recv_sem)

    anti = (r, c, o)
    up, down = (r - 1, c, h), (r + 1, c, h)
    left, right = (r, c - 1, h), (r, c + 1, h)
    sibling = (r, zl * 2 + 1 - core, h)
    partner = (r, (levels - 1 - zl) * 2 + core, o)
    has_up, has_down, has_left, has_right = r > 0, r < rows - 1, c > 0, c < cols - 1
    border = (zl == 0) | (zl == levels - 1)
    lower = zl < levels // 2
    outer_z = jnp.where(lower, zl - 1, zl + 1)
    inner_z = jnp.where(lower, zl + 1, zl - 1)
    outer, inner = (r, outer_z * 2 + core, h), (r, inner_z * 2 + core, h)
    has_outer = jnp.logical_not(border)
    has_inner = (zl != levels // 2 - 1) & (zl != levels // 2)

    def ring_x(d):
        return (lax.rem(px + d + side, side) * side + py, c, h)

    def ring_y(d):
        return (px * side + lax.rem(py + d + side, side), c, h)

    barrier = pltpu.get_barrier_semaphore()
    always = [anti, ring_x(1), ring_x(-1), ring_y(1), ring_y(-1)]
    sometimes = [
        (has_up, up), (has_down, down), (has_left, left), (has_right, right),
        (border, partner), (has_outer, outer), (has_inner, inner),
    ]
    for device in always:
        pl.semaphore_signal(barrier, inc=1, device_id=device, device_id_type=MESH)
    count = len(always)
    for there, device in sometimes:
        count = count + jnp.where(there, 1, 0)

        @pl.when(there)
        def _():
            pl.semaphore_signal(barrier, inc=1, device_id=device, device_id_type=MESH)

    locals_ = [
        pltpu.make_async_copy(img, x.at[1, h, pl.ds(2, TILE)], local_sem.at[0]),
        pltpu.make_async_copy(w1_own, w1.at[h], local_sem.at[1]),
        pltpu.make_async_copy(w2_own, w2, local_sem.at[2]),
    ]
    for copy in locals_:
        copy.start()
    s1all[h] = s1[...]
    t1all[h] = t1[...]
    strip[...] = jnp.zeros_like(strip)
    edge[...] = jnp.zeros_like(edge)

    @pl.when(jnp.logical_not(has_up))
    def _():
        x[1, :, 0:2] = jnp.zeros((2, 2, TILE, HALF), BF16)

    @pl.when(jnp.logical_not(has_down))
    def _():
        x[1, :, EXT - 2 : EXT] = jnp.zeros((2, 2, TILE, HALF), BF16)

    pl.semaphore_wait(barrier, count)

    part = TAPS // 2 // rows
    block = part * side
    my_half, its_half = core * (TAPS // 2), (1 - core) * (TAPS // 2)

    def w_rows(start, size):
        return w1.at[o, pl.ds(pl.multiple_of(start, 16), size)]

    piece = my_half + r * part
    chain_in = sems.copy(
        w1_own.at[pl.ds(pl.multiple_of(piece, 16), part)],
        w1.at[h, pl.ds(pl.multiple_of(piece, 16), part)],
        partner,
    )

    @pl.when(border)
    def _():
        chain_in.start()

    scale_copy = sems.copy(s1, s1all.at[h], anti)
    shift_copy = sems.copy(t1, t1all.at[h], anti)
    scale_copy.start()
    shift_copy.start()
    across = [
        sems.copy(img.at[pl.ds(r0, n)], x.at[1, h, pl.ds(r0 + 2, n)], anti) for r0, n in CHUNKS
    ]
    for copy in across[:2]:
        copy.start()

    def row_copies(half, source):
        top = sems.copy(source(0), x.at[1, half, pl.ds(EXT - 2, 2)], up)
        bottom = sems.copy(source(TILE - 2), x.at[1, half, pl.ds(0, 2)], down)
        return top, bottom

    own_top, own_bottom = row_copies(h, lambda row: img.at[pl.ds(row, 2)])
    its_top, its_bottom = row_copies(o, lambda row: x.at[1, o, pl.ds(row + 2, 2)])

    @pl.when(has_up)
    def _():
        own_top.start()

    @pl.when(has_down)
    def _():
        own_bottom.start()

    column = lax.broadcasted_iota(jnp.int32, (TILE, HALF), 0)

    def extract(half, e0, n):
        @pl.loop(e0, e0 + n)
        def _(e):
            tile = x[1, half, e].astype(F32)
            here = pl.ds(e, 1)
            strip[0, 2, half, here, :] = tile[0:1]
            strip[1, 0, half, here, :] = tile[TILE - 1 : TILE]
            edge[0, 0, half, here, :] = tile[0:1]
            edge[0, 1, half, here, :] = tile[1:2]
            edge[1, 0, half, here, :] = tile[TILE - 2 : TILE - 1]
            edge[1, 1, half, here, :] = tile[TILE - 1 : TILE]

    def pack(half, e0, padded, send):
        for d in range(2):
            both = [edge[d, i, half, e0 : e0 + padded, :] for i in range(2)]
            send[d] = jnp.concatenate(both, axis=0).astype(BF16)

    def column_copies(send, land):
        return sems.copy(send.at[0], land.at[1], left), sems.copy(send.at[1], land.at[0], right)

    def start_columns(copies):
        @pl.when(has_left)
        def _():
            copies[0].start()

        @pl.when(has_right)
        def _():
            copies[1].start()

    def unpack(half, e0, n, padded, land, copies):
        @pl.when(has_left)
        def _():
            copies[1].wait_recv()
            got = land[0].astype(F32)
            strip[0, 0, half, e0 : e0 + n, :] = got[0:n]
            strip[0, 1, half, e0 : e0 + n, :] = got[padded : padded + n]

        @pl.when(has_right)
        def _():
            copies[0].wait_recv()
            got = land[1].astype(F32)
            strip[1, 1, half, e0 : e0 + n, :] = got[0:n]
            strip[1, 2, half, e0 : e0 + n, :] = got[padded : padded + n]

    def shift_columns(half, e0, n):
        @pl.loop(e0, e0 + n)
        def _(e):
            tile = x[1, half, e].astype(F32)
            before, after = strip[0, 1, half, pl.ds(e, 1), :], strip[1, 1, half, pl.ds(e, 1), :]
            x[0, half, e] = jnp.where(column == 0, before, pltpu.roll(tile, 1, 0)).astype(BF16)
            x[2, half, e] = jnp.where(column == TILE - 1, after, pltpu.roll(tile, TILE - 1, 0)).astype(BF16)

    small = [column_copies(msg_out.at[i], msg_in.at[i]) for i in range(len(GROUPS))]
    large = column_copies(big_out, big_in)

    def give(slot, half):
        e0, n = GROUPS[slot]
        extract(half, e0, n)
        pack(half, e0, 8, msg_out.at[slot])
        start_columns(small[slot])

    def take(slot, half):
        e0, n = GROUPS[slot]
        unpack(half, e0, n, 8, msg_in.at[slot], small[slot])
        shift_columns(half, e0, n)

    keep_left, keep_right = jnp.where(has_left, 1.0, 0.0), jnp.where(has_right, 1.0, 0.0)

    def conv_one(q0, n, half):
        total = None
        for a in range(3):
            for b in range(3):
                for i in range(2):
                    e0 = q0 + a
                    main = x[b, i, e0 : e0 + n].reshape(n * TILE, HALF)
                    sides = [strip[s, b, i, e0 : e0 + 8, :] for s in range(2)]
                    sides = jnp.concatenate(sides, axis=0).astype(BF16)
                    k = ((a * 3 + b) * 2 + i) * HALF
                    term = jnp.dot(
                        jnp.concatenate([main, sides], axis=0), w1[half, k : k + HALF, :], preferred_element_type=F32
                    )
                    total = term if total is None else total + term
        acc[0 : n * TILE + 16, :] = jnp.maximum(total * s1all[half] + t1all[half], 0.0)

        @pl.loop(0, n)
        def _(i):
            q = q0 + i
            outside = ((q == 0) & jnp.logical_not(has_up)) | ((q == HID - 1) & jnp.logical_not(has_down))
            keep = jnp.where(outside, 0.0, 1.0)
            tile = acc[pl.ds(pl.multiple_of(i * TILE, TILE), TILE), :] * keep
            before = acc[pl.ds(n * TILE + i, 1), :] * (keep * keep_left)
            after = acc[pl.ds(n * TILE + 8 + i, 1), :] * (keep * keep_right)
            hid[0, half, q] = jnp.where(column == 0, before, pltpu.roll(tile, 1, 0)).astype(BF16)
            hid[1, half, q] = tile.astype(BF16)
            hid[2, half, q] = jnp.where(column == TILE - 1, after, pltpu.roll(tile, TILE - 1, 0)).astype(BF16)

    out_copies = []

    def conv_two(i0, n):
        total = None
        for a in range(3):
            for b in range(3):
                for i in range(2):
                    main = hid[b, i, i0 + a : i0 + a + n].reshape(n * TILE, HALF)
                    k = ((a * 3 + b) * 2 + i) * HALF
                    term = jnp.dot(main, w2[k : k + HALF, :], preferred_element_type=F32)
                    total = term if total is None else total + term
        done = jnp.maximum(total * s2[...] + t2[...], 0.0).astype(BF16)
        result[i0 : i0 + n] = done.reshape(n, TILE, HALF)
        copy = pltpu.make_async_copy(
            result.at[pl.ds(i0, n)], out.at[pl.ds(i0, n)], out_sem.at[len(out_copies)]
        )
        copy.start()
        out_copies.append(copy)

    locals_[0].wait()
    extract(h, 2, TILE)
    pack(h, 2, TILE, big_out)
    start_columns(large)

    @pl.when(has_up)
    def _():
        own_bottom.wait_recv()

    give(OWN_TOP, h)

    @pl.when(has_down)
    def _():
        own_top.wait_recv()

    give(OWN_BOTTOM, h)

    chain_in.wait_recv()
    chain_on = pltpu.make_async_remote_copy(
        w_rows(piece, part), w_rows(piece, part), send_sem.at[sems.used], recv_sem.at[0],
        device_id=inner, device_id_type=MESH,
    )
    sems.used += 1

    @pl.when(has_inner)
    def _():
        chain_on.start()

    def y_piece(d):
        return w_rows(my_half + px * block + lax.rem(py + d + side, side) * part, part)

    def x_block(d, lo=0, hi=block):
        return w_rows(my_half + lax.rem(px + d + side, side) * block + lo, hi - lo)

    def same(ref, device):
        return sems.copy(ref, ref, device)

    y_on = same(y_piece(0), ring_y(1)), same(y_piece(0), ring_y(-1))
    for copy in y_on:
        copy.start()

    unpack(h, 2, TILE, TILE, big_in, large)
    shift_columns(h, 2, TILE)
    take(OWN_TOP, h)
    take(OWN_BOTTOM, h)

    for copy in across[2:]:
        copy.start()

    y_on[0].wait_recv()
    y_far = same(y_piece(-1), ring_y(1))
    y_far.start()
    y_on[1].wait_recv()
    y_far.wait_recv()
    x_on = same(x_block(0), ring_x(1)), same(x_block(0), ring_x(-1))
    for copy in x_on:
        copy.start()
    to_sibling = [same(x_block(d), sibling) for d in (0, -1, 1, 2)]
    to_sibling[0].start()

    across[0].wait_recv()

    @pl.when(has_up)
    def _():
        its_top.start()

    give(CHUNK_SLOT, o)

    x_on[0].wait_recv()
    x_far = same(x_block(-1, 0, block // 2), ring_x(1)), same(x_block(1, block // 2, block), ring_x(-1))
    x_far[0].start()
    to_sibling[1].start()
    x_on[1].wait_recv()
    x_far[1].start()
    to_sibling[2].start()

    across[1].wait_recv()

    @pl.when(has_down)
    def _():
        its_bottom.start()

    give(CHUNK_SLOT + 1, o)

    for copy in x_far:
        copy.wait_recv()
    to_sibling[3].start()

    @pl.when(has_up)
    def _():
        its_bottom.wait_recv()

    give(TOP, o)

    @pl.when(has_down)
    def _():
        its_top.wait_recv()

    give(BOTTOM, o)
    take(CHUNK_SLOT, o)
    take(TOP, o)
    take(CHUNK_SLOT + 1, o)
    take(BOTTOM, o)
    for copy in locals_[1:]:
        copy.wait()
    conv_one(0, 8, h)
    conv_one(26, 8, h)
    for copy in to_sibling:
        copy.wait_recv()
    scale_copy.wait_recv()
    shift_copy.wait_recv()
    conv_one(0, 8, o)
    conv_one(26, 8, o)
    conv_two(0, 6)
    conv_two(26, 6)

    for i, (q0, n, i0, m) in enumerate(((8, 8, 6, 8), (16, 4, 14, 4), (20, 6, 18, 8))):
        across[2 + i].wait_recv()
        give(CHUNK_SLOT + 2 + i, o)
        take(CHUNK_SLOT + 2 + i, o)
        conv_one(q0, n, h)
        conv_one(q0, n, o)
        conv_two(i0, m)

    for copy in (scale_copy, shift_copy, *across, *y_on, y_far, *x_on, *x_far, *to_sibling):
        copy.wait_send()
    pairs = [(border, chain_in), (has_inner, chain_on)]
    pairs += [(has_up, own_top), (has_down, own_bottom), (has_up, its_top), (has_down, its_bottom)]
    for copies in (*small, large):
        pairs += [(has_left, copies[0]), (has_right, copies[1])]
    for there, copy in pairs:

        @pl.when(there)
        def _():
            copy.wait_send()

    for copy in out_copies:
        copy.wait()


def shards(rows, cols, image, weight_one, scale_one, shift_one, weight_two, scale_two, shift_two):
    def body(*refs):
        kernel(rows, cols, *refs)

    vmem, anywhere = pl.BlockSpec(memory_space=pltpu.VMEM), pl.BlockSpec(memory_space=pl.ANY)
    flops = 2 * TILE * TILE * TAPS * HALF * 3
    return pl.pallas_call(
        body,
        name="two_convolutions",
        out_shape=jax.ShapeDtypeStruct((TILE, TILE, HALF), BF16),
        in_specs=[anywhere, anywhere, vmem, vmem, anywhere, vmem, vmem],
        out_specs=anywhere,
        scratch_shapes=[
            pltpu.VMEM((3, 2, EXT, TILE, HALF), BF16),
            pltpu.VMEM((3, 2, HID, TILE, HALF), BF16),
            pltpu.VMEM((2, TAPS, HALF), BF16),
            pltpu.VMEM((TAPS, HALF), BF16),
            pltpu.VMEM((2, 3, 2, 48, HALF), F32),
            pltpu.VMEM((2, 2, 2, 48, HALF), F32),
            pltpu.VMEM((len(GROUPS), 2, 16, HALF), BF16),
            pltpu.VMEM((len(GROUPS), 2, 16, HALF), BF16),
            pltpu.VMEM((2, 2 * TILE, HALF), BF16),
            pltpu.VMEM((2, 2 * TILE, HALF), BF16),
            pltpu.VMEM((8 * TILE + 16, HALF), F32),
            pltpu.VMEM((TILE, TILE, HALF), BF16),
            pltpu.VMEM((2, 1, HALF), F32),
            pltpu.VMEM((2, 1, HALF), F32),
            pltpu.SemaphoreType.DMA((N_SEMS,)),
            pltpu.SemaphoreType.DMA((N_SEMS,)),
            pltpu.SemaphoreType.DMA((3,)),
            pltpu.SemaphoreType.DMA((8,)),
        ],
        compiler_params=pltpu.CompilerParams(
            collective_id=0, has_side_effects=True, vmem_limit_bytes=48 * 1024 * 1024
        ),
        cost_estimate=pl.CostEstimate(flops=flops, bytes_accessed=6_000_000, transcendentals=0),
    )(
        image,
        weight_one.reshape(TAPS, HALF),
        scale_one.reshape(1, HALF),
        shift_one.reshape(1, HALF),
        weight_two.reshape(TAPS, HALF),
        scale_two.reshape(1, HALF),
        shift_two.reshape(1, HALF),
    )


def solution(mesh):
    rows, cols = mesh.shape["row"], mesh.shape["col"]

    def local(*arrays):
        return shards(rows, cols, *arrays)

    return jax.shard_map(
        local,
        mesh=mesh,
        in_specs=(
            P("row", "col", "ch"),
            P(None, None, None, "ch"),
            P("ch"),
            P("ch"),
            P(None, None, None, "ch"),
            P("ch"),
            P("ch"),
        ),
        out_specs=P("row", "col", "ch"),
        check_vma=False,
    )
```

time: 217 us -> 118 us (0.54)
  the two profiles are of different devices: /device:TPU:89 before, /device:TPU:146 now
where the time goes in v1:
time: 118 us; the launch traced here: 117 us
  Pallas kernels  109 us (92%)
  local copies, waits for them, and re-layouts  7.88 us (7%)
    pallas_call x1, Pallas kernels, shards(): pl.pallas_call(body, name='two_convolutions', out_shape=jax.ShapeDtypeStr...  109 us
    unnamed x15, local copies, waits for them, and re-layouts  7.88 us

profile of v1, /device:TPU:146, one launch (start us, length us, event | category | flops | bytes accessed | tf_op | source)
XLA Modules:
  0.0 117.4 jit_solution(17153534578886658150)
XLA Ops:
  0.0 0.0 copy-start
  0.0 1.7 %copy-done = bf16[3,3,512,256]{3,2,1,0:T(8,128)(2,1)S(1)} copy-done((bf16[3,3,512,256]{3,2,1,0:T(8,128)(2,1)S(1)}, bf16[3,3,512,256]{3,2,1,0:T(8,128)(2,1)}, u32[]{:S(2)}) %copy-start) | copy-done | bytes 2359320
  1.7 0.0 copy-start.1
  1.7 1.7 %copy-done.1 = bf16[3,3,512,256]{3,2,1,0:T(8,128)(2,1)S(1)} copy-done((bf16[3,3,512,256]{3,2,1,0:T(8,128)(2,1)S(1)}, bf16[3,3,512,256]{3,2,1,0:T(8,128)(2,1)}, u32[]{:S(2)}) %copy-start.1) | copy-done | bytes 2359320
  3.3 0.0 copy-start.2
  3.3 1.0 copy-done.2
  4.4 0.0 copy-start.3
  4.4 0.7 copy-done.3
  5.1 0.0 copy-start.4
  5.1 0.7 copy-done.4
  5.7 0.0 copy-start.5
  5.7 0.7 copy-done.5
  6.4 0.0 copy-start.6
  6.4 0.7 copy-done.6
  7.1 109.5 %two_convolutions.1 = bf16[32,32,256]{2,1,0:T(8,128)(2,1)S(1)} custom-call(bf16[32,32,256]{2,1,0:T(8,128)(2,1)S(1)} %copy-done.2, bf16[4608,256]{1,0:T(8,128)(2,1)S(1)} %bitcast.6, f32[1,256]{1,0:T(1,128)S(1)} %bitcast.8, f32[1,256]{1,0:T(1,128)S(1)} %bitcast.9, bf16[4608,256]{1,0:T(8,128)(2,1)S(1)} %bitcast.7, f32[1,256]{1,0:T(1,128)S(1)} %bitcast.10, ...), custom_call_target="tpu_custom_call" | custom-call | flops 7247757312 | bytes 6000000 | tf_op jit(solution)/shard_map/two_convolutions/pallas_call | solution.py:418
  116.6 0.8 copy.9
Async XLA Ops:
  0.0 1.7 %copy-start = (bf16[3,3,512,256]{3,2,1,0:T(8,128)(2,1)S(1)}, bf16[3,3,512,256]{3,2,1,0:T(8,128)(2,1)}, u32[]{:S(2)}) copy-start(bf16[3,3,512,256]{3,2,1,0:T(8,128)(2,1)} %param.8) | copy-start | bytes 7077892
  1.7 1.7 %copy-start.1 = (bf16[3,3,512,256]{3,2,1,0:T(8,128)(2,1)S(1)}, bf16[3,3,512,256]{3,2,1,0:T(8,128)(2,1)}, u32[]{:S(2)}) copy-start(bf16[3,3,512,256]{3,2,1,0:T(8,128)(2,1)} %param.11) | copy-start | bytes 7077892
  3.3 1.0 copy-start.2
  4.4 0.7 copy-start.3
  5.1 0.7 copy-start.4
  5.7 0.7 copy-start.5
  6.4 0.7 copy-start.6

commit v2 on v1

--- a/solution.py
+++ b/solution.py
@@ -32,15 +32,48 @@
         )
 
 
-N_SEMS = 48
+class Parts:
+    def __init__(self, sems, source, target, start, size, parts, device):
+        self.whole = sems.copy(rows_of(source, start, size), rows_of(target, start, size), device)
+        self.cuts = [
+            pltpu.make_async_remote_copy(
+                rows_of(source, start + i * (size // parts), size // parts),
+                rows_of(target, start + i * (size // parts), size // parts),
+                sems.send.at[sems.used - 1],
+                sems.recv.at[sems.used - 1],
+                device_id=device,
+                device_id_type=MESH,
+            )
+            for i in range(parts)
+        ]
+
+    def start(self):
+        for cut in self.cuts:
+            cut.start()
+
+    def wait_recv(self):
+        self.whole.wait_recv()
+
+    def wait_send(self):
+        self.whole.wait_send()
+
+
+def rows_of(ref, start, size):
+    return ref.at[pl.ds(pl.multiple_of(start, 16), size)]
+
+
+N_SEMS = 64
+UNIT = 2
+AHEAD = 2
+FIRST = 3
 
 
 def kernel(
     rows, cols,
     img, w1_own, s1, t1, w2_own, s2, t2,
     out,
-    x, hid, w1, w2, strip, edge, msg_out, msg_in, big_out, big_in, acc, result, s1all, t1all,
-    send_sem, recv_sem, local_sem, out_sem,
+    x, hid, w1, w2, strip, edge, msg_out, msg_in, big_out, big_in, result, s1all, t1all, s2in, t2in,
+    send_sem, recv_sem, unit_sem, local_sem, out_sem,
 ):
     r, c, h = lax.axis_index("row"), lax.axis_index("col"), lax.axis_index("ch")
     o = 1 - h
@@ -61,8 +94,9 @@
     outer_z = jnp.where(lower, zl - 1, zl + 1)
     inner_z = jnp.where(lower, zl + 1, zl - 1)
     outer, inner = (r, outer_z * 2 + core, h), (r, inner_z * 2 + core, h)
-    has_outer = jnp.logical_not(border)
-    has_inner = (zl != levels // 2 - 1) & (zl != levels // 2)
+    hop = jnp.where(lower, zl, levels - 1 - zl)
+    has_outer, has_inner = hop == 1, border
+    straight = hop >= 2
 
     def ring_x(d):
         return (lax.rem(px + d + side, side) * side + py, c, h)
@@ -71,7 +105,7 @@
         return (px * side + lax.rem(py + d + side, side), c, h)
 
     barrier = pltpu.get_barrier_semaphore()
-    always = [anti, ring_x(1), ring_x(-1), ring_y(1), ring_y(-1)]
+    always = [anti, *(ring_x(d) for d in (1, -1, 2)), *(ring_y(d) for d in (1, -1, 2))]
     sometimes = [
         (has_up, up), (has_down, down), (has_left, left), (has_right, right),
         (border, partner), (has_outer, outer), (has_inner, inner),
@@ -90,11 +124,13 @@
         pltpu.make_async_copy(img, x.at[1, h, pl.ds(2, TILE)], local_sem.at[0]),
         pltpu.make_async_copy(w1_own, w1.at[h], local_sem.at[1]),
         pltpu.make_async_copy(w2_own, w2, local_sem.at[2]),
+        pltpu.make_async_copy(s1, s1all.at[h], local_sem.at[3]),
+        pltpu.make_async_copy(t1, t1all.at[h], local_sem.at[4]),
+        pltpu.make_async_copy(s2, s2in, local_sem.at[5]),
+        pltpu.make_async_copy(t2, t2in, local_sem.at[6]),
     ]
     for copy in locals_:
         copy.start()
-    s1all[h] = s1[...]
-    t1all[h] = t1[...]
     strip[...] = jnp.zeros_like(strip)
     edge[...] = jnp.zeros_like(edge)
 
@@ -105,52 +141,6 @@
     @pl.when(jnp.logical_not(has_down))
     def _():
         x[1, :, EXT - 2 : EXT] = jnp.zeros((2, 2, TILE, HALF), BF16)
-
-    pl.semaphore_wait(barrier, count)
-
-    part = TAPS // 2 // rows
-    block = part * side
-    my_half, its_half = core * (TAPS // 2), (1 - core) * (TAPS // 2)
-
-    def w_rows(start, size):
-        return w1.at[o, pl.ds(pl.multiple_of(start, 16), size)]
-
-    piece = my_half + r * part
-    chain_in = sems.copy(
-        w1_own.at[pl.ds(pl.multiple_of(piece, 16), part)],
-        w1.at[h, pl.ds(pl.multiple_of(piece, 16), part)],
-        partner,
-    )
-
-    @pl.when(border)
-    def _():
-        chain_in.start()
-
-    scale_copy = sems.copy(s1, s1all.at[h], anti)
-    shift_copy = sems.copy(t1, t1all.at[h], anti)
-    scale_copy.start()
-    shift_copy.start()
-    across = [
-        sems.copy(img.at[pl.ds(r0, n)], x.at[1, h, pl.ds(r0 + 2, n)], anti) for r0, n in CHUNKS
-    ]
-    for copy in across[:2]:
-        copy.start()
-
-    def row_copies(half, source):
-        top = sems.copy(source(0), x.at[1, half, pl.ds(EXT - 2, 2)], up)
-        bottom = sems.copy(source(TILE - 2), x.at[1, half, pl.ds(0, 2)], down)
-        return top, bottom
-
-    own_top, own_bottom = row_copies(h, lambda row: img.at[pl.ds(row, 2)])
-    its_top, its_bottom = row_copies(o, lambda row: x.at[1, o, pl.ds(row + 2, 2)])
-
-    @pl.when(has_up)
-    def _():
-        own_top.start()
-
-    @pl.when(has_down)
-    def _():
-        own_bottom.start()
 
     column = lax.broadcasted_iota(jnp.int32, (TILE, HALF), 0)
 
@@ -205,9 +195,6 @@
             before, after = strip[0, 1, half, pl.ds(e, 1), :], strip[1, 1, half, pl.ds(e, 1), :]
             x[0, half, e] = jnp.where(column == 0, before, pltpu.roll(tile, 1, 0)).astype(BF16)
             x[2, half, e] = jnp.where(column == TILE - 1, after, pltpu.roll(tile, TILE - 1, 0)).astype(BF16)
-
-    small = [column_copies(msg_out.at[i], msg_in.at[i]) for i in range(len(GROUPS))]
-    large = column_copies(big_out, big_in)
 
     def give(slot, half):
         e0, n = GROUPS[slot]
@@ -236,16 +223,15 @@
                         jnp.concatenate([main, sides], axis=0), w1[half, k : k + HALF, :], preferred_element_type=F32
                     )
                     total = term if total is None else total + term
-        acc[0 : n * TILE + 16, :] = jnp.maximum(total * s1all[half] + t1all[half], 0.0)
-
-        @pl.loop(0, n)
-        def _(i):
+        value = jnp.maximum(total * s1all[half] + t1all[half], 0.0)
+        for i in range(n):
             q = q0 + i
-            outside = ((q == 0) & jnp.logical_not(has_up)) | ((q == HID - 1) & jnp.logical_not(has_down))
-            keep = jnp.where(outside, 0.0, 1.0)
-            tile = acc[pl.ds(pl.multiple_of(i * TILE, TILE), TILE), :] * keep
-            before = acc[pl.ds(n * TILE + i, 1), :] * (keep * keep_left)
-            after = acc[pl.ds(n * TILE + 8 + i, 1), :] * (keep * keep_right)
+            tile = value[i * TILE : (i + 1) * TILE]
+            before = value[n * TILE + i : n * TILE + i + 1] * keep_left
+            after = value[n * TILE + 8 + i : n * TILE + 9 + i] * keep_right
+            if q in (0, HID - 1):
+                keep = jnp.where(has_up if q == 0 else has_down, 1.0, 0.0)
+                tile, before, after = tile * keep, before * keep, after * keep
             hid[0, half, q] = jnp.where(column == 0, before, pltpu.roll(tile, 1, 0)).astype(BF16)
             hid[1, half, q] = tile.astype(BF16)
             hid[2, half, q] = jnp.where(column == TILE - 1, after, pltpu.roll(tile, TILE - 1, 0)).astype(BF16)
@@ -261,7 +247,7 @@
                     k = ((a * 3 + b) * 2 + i) * HALF
                     term = jnp.dot(main, w2[k : k + HALF, :], preferred_element_type=F32)
                     total = term if total is None else total + term
-        done = jnp.maximum(total * s2[...] + t2[...], 0.0).astype(BF16)
+        done = jnp.maximum(total * s2in[...] + t2in[...], 0.0).astype(BF16)
         result[i0 : i0 + n] = done.reshape(n, TILE, HALF)
         copy = pltpu.make_async_copy(
             result.at[pl.ds(i0, n)], out.at[pl.ds(i0, n)], out_sem.at[len(out_copies)]
@@ -272,8 +258,85 @@
     locals_[0].wait()
     extract(h, 2, TILE)
     pack(h, 2, TILE, big_out)
+
+    pl.semaphore_wait(barrier, count)
+
+    part = TAPS // 2 // rows
+    block = part * side
+    my_half = core * (TAPS // 2)
+    near_pos, far_pos = jnp.where(core == 0, py, px), jnp.where(core == 0, px, py)
+    piece = my_half + far_pos * block + near_pos * part
+
+    def ring(d, first):
+        along_y = (core == 0) if first else (core == 1)
+        qx = jnp.where(along_y, px, lax.rem(px + d + side, side))
+        qy = jnp.where(along_y, lax.rem(py + d + side, side), py)
+        return (qx * side + qy, c, h)
+
+    chain_in = Parts(sems, w1_own, w1.at[h], piece, part, 3, partner)
+    chain_on = Parts(Sems(send_sem.at[pl.ds(sems.used, 1)], recv_sem.at[pl.ds(0, 1)]), w1.at[o], w1.at[o], piece, part, 3, inner)
+    sems.used += 1
+
+    chain_far = Parts(Sems(send_sem.at[pl.ds(sems.used, 1)], recv_sem.at[pl.ds(0, 1)]), w1_own, w1.at[h], piece, part, 3, anti)
+    sems.used += 1
+
+    @pl.when(border)
+    def _():
+        chain_in.start()
+
+    @pl.when(straight)
+    def _():
+        chain_far.start()
+
+    scale_copy = sems.copy(s1, s1all.at[h], anti)
+    shift_copy = sems.copy(t1, t1all.at[h], anti)
+    scale_copy.start()
+    shift_copy.start()
+
+    def row_copies(half, source):
+        top = sems.copy(source(0), x.at[1, half, pl.ds(EXT - 2, 2)], up)
+        bottom = sems.copy(source(TILE - 2), x.at[1, half, pl.ds(0, 2)], down)
+        return top, bottom
+
+    own_top, own_bottom = row_copies(h, lambda row: img.at[pl.ds(row, 2)])
+    its_top, its_bottom = row_copies(o, lambda row: x.at[1, o, pl.ds(row + 2, 2)])
+
+    @pl.when(has_up)
+    def _():
+        own_top.start()
+
+    @pl.when(has_down)
+    def _():
+        own_bottom.start()
+
+    small = [column_copies(msg_out.at[i], msg_in.at[i]) for i in range(len(GROUPS))]
+    large = column_copies(big_out, big_in)
     start_columns(large)
 
+    across, units = [], []
+    for r0, n in CHUNKS:
+        chunk = sems.copy(img.at[pl.ds(r0, n)], x.at[1, h, pl.ds(r0 + 2, n)], anti)
+        across.append(chunk)
+        for row in range(r0, r0 + n, UNIT):
+            sem = sems.used - 1
+            units.append(
+                pltpu.make_async_remote_copy(
+                    img.at[pl.ds(row, UNIT)], x.at[1, h, pl.ds(row + 2, UNIT)],
+                    unit_sem.at[len(units)], recv_sem.at[sem], device_id=anti, device_id_type=MESH,
+                )
+            )
+    sent = [0]
+
+    def pump(n):
+        for _ in range(n * 2 // UNIT):
+            if sent[0] < len(units):
+                if sent[0] >= AHEAD:
+                    units[sent[0] - AHEAD].wait_send()
+                units[sent[0]].start()
+                sent[0] += 1
+
+    pump(FIRST)
+
     @pl.when(has_up)
     def _():
         own_bottom.wait_recv()
@@ -286,48 +349,47 @@
 
     give(OWN_BOTTOM, h)
 
-    chain_in.wait_recv()
-    chain_on = pltpu.make_async_remote_copy(
-        w_rows(piece, part), w_rows(piece, part), send_sem.at[sems.used], recv_sem.at[0],
-        device_id=inner, device_id_type=MESH,
-    )
-    sems.used += 1
-
-    @pl.when(has_inner)
-    def _():
-        chain_on.start()
-
-    def y_piece(d):
-        return w_rows(my_half + px * block + lax.rem(py + d + side, side) * part, part)
-
-    def x_block(d, lo=0, hi=block):
-        return w_rows(my_half + lax.rem(px + d + side, side) * block + lo, hi - lo)
-
-    def same(ref, device):
-        return sems.copy(ref, ref, device)
-
-    y_on = same(y_piece(0), ring_y(1)), same(y_piece(0), ring_y(-1))
-    for copy in y_on:
-        copy.start()
-
+    mine = my_half + far_pos * block
+    first_on = [Parts(sems, w1.at[o], w1.at[o], piece, part, 3, ring(d, True)) for d in (1, -1, 2)]
+    second_on = [Parts(sems, w1.at[o], w1.at[o], mine, block, 4, ring(d, False)) for d in (1, -1, 2)]
+    near = Parts(sems, w1.at[o], w1.at[o], mine, block, 4, sibling)
+    far = [
+        Parts(sems, w1.at[o], w1.at[o], my_half + lax.rem(far_pos + d + side, side) * block, block, 4, sibling)
+        for d in (-1, 1, 2)
+    ]
+
+    def weights_here():
+        chain_in.wait_recv()
+
+        @pl.when(has_inner)
+        def _():
+            chain_on.start()
+
+        for copy in first_on:
+            copy.start()
+
+    @pl.when(border)
+    def _():
+        weights_here()
+
+    pump(1)
+
+    @pl.when(jnp.logical_not(border))
+    def _():
+        weights_here()
+
+    pump(1)
     unpack(h, 2, TILE, TILE, big_in, large)
     shift_columns(h, 2, TILE)
     take(OWN_TOP, h)
     take(OWN_BOTTOM, h)
-
-    for copy in across[2:]:
+    pump(1)
+    for copy in first_on:
+        copy.wait_recv()
+    for copy in second_on:
         copy.start()
-
-    y_on[0].wait_recv()
-    y_far = same(y_piece(-1), ring_y(1))
-    y_far.start()
-    y_on[1].wait_recv()
-    y_far.wait_recv()
-    x_on = same(x_block(0), ring_x(1)), same(x_block(0), ring_x(-1))
-    for copy in x_on:
-        copy.start()
-    to_sibling = [same(x_block(d), sibling) for d in (0, -1, 1, 2)]
-    to_sibling[0].start()
+    near.start()
+    pump(1)
 
     across[0].wait_recv()
 
@@ -336,15 +398,7 @@
         its_top.start()
 
     give(CHUNK_SLOT, o)
-
-    x_on[0].wait_recv()
-    x_far = same(x_block(-1, 0, block // 2), ring_x(1)), same(x_block(1, block // 2, block), ring_x(-1))
-    x_far[0].start()
-    to_sibling[1].start()
-    x_on[1].wait_recv()
-    x_far[1].start()
-    to_sibling[2].start()
-
+    pump(4)
     across[1].wait_recv()
 
     @pl.when(has_down)
@@ -352,10 +406,9 @@
         its_bottom.start()
 
     give(CHUNK_SLOT + 1, o)
-
-    for copy in x_far:
+    for copy, on in zip(second_on, far):
         copy.wait_recv()
-    to_sibling[3].start()
+        on.start()
 
     @pl.when(has_up)
     def _():
@@ -368,34 +421,52 @@
         its_top.wait_recv()
 
     give(BOTTOM, o)
+    pump(1)
     take(CHUNK_SLOT, o)
     take(TOP, o)
-    take(CHUNK_SLOT + 1, o)
-    take(BOTTOM, o)
     for copy in locals_[1:]:
         copy.wait()
     conv_one(0, 8, h)
+    pump(1)
+    take(CHUNK_SLOT + 1, o)
+    take(BOTTOM, o)
     conv_one(26, 8, h)
-    for copy in to_sibling:
-        copy.wait_recv()
+    pump(1)
     scale_copy.wait_recv()
     shift_copy.wait_recv()
+    pump(1)
+    for copy in (near, *far):
+        copy.wait_recv()
     conv_one(0, 8, o)
+    pump(1)
+    conv_two(0, 6)
+    pump(1)
     conv_one(26, 8, o)
-    conv_two(0, 6)
+    pump(1)
     conv_two(26, 6)
-
-    for i, (q0, n, i0, m) in enumerate(((8, 8, 6, 8), (16, 4, 14, 4), (20, 6, 18, 8))):
-        across[2 + i].wait_recv()
-        give(CHUNK_SLOT + 2 + i, o)
-        take(CHUNK_SLOT + 2 + i, o)
-        conv_one(q0, n, h)
-        conv_one(q0, n, o)
-        conv_two(i0, m)
-
-    for copy in (scale_copy, shift_copy, *across, *y_on, y_far, *x_on, *x_far, *to_sibling):
+    pump(len(units))
+    last = CHUNK_SLOT + 2
+    across[2].wait_recv()
+    give(last, o)
+    across[3].wait_recv()
+    give(last + 1, o)
+    take(last, o)
+    conv_one(8, 8, h)
+    across[4].wait_recv()
+    give(last + 2, o)
+    conv_one(8, 8, o)
+    take(last + 1, o)
+    conv_one(16, 4, h)
+    conv_one(16, 4, o)
+    conv_two(6, 12)
+    take(last + 2, o)
+    conv_one(20, 6, h)
+    conv_one(20, 6, o)
+    conv_two(18, 8)
+
+    for copy in (scale_copy, shift_copy, *units[-AHEAD:], *first_on, *second_on, near, *far):
         copy.wait_send()
-    pairs = [(border, chain_in), (has_inner, chain_on)]
+    pairs = [(border, chain_in), (straight, chain_far), (has_inner, chain_on)]
     pairs += [(has_up, own_top), (has_down, own_bottom), (has_up, its_top), (has_down, its_bottom)]
     for copies in (*small, large):
         pairs += [(has_left, copies[0]), (has_right, copies[1])]
@@ -413,14 +484,14 @@
     def body(*refs):
         kernel(rows, cols, *refs)
 
-    vmem, anywhere = pl.BlockSpec(memory_space=pltpu.VMEM), pl.BlockSpec(memory_space=pl.ANY)
+    hbm = pl.BlockSpec(memory_space=pltpu.HBM)
     flops = 2 * TILE * TILE * TAPS * HALF * 3
     return pl.pallas_call(
         body,
         name="two_convolutions",
         out_shape=jax.ShapeDtypeStruct((TILE, TILE, HALF), BF16),
-        in_specs=[anywhere, anywhere, vmem, vmem, anywhere, vmem, vmem],
-        out_specs=anywhere,
+        in_specs=[hbm] * 7,
+        out_specs=hbm,
         scratch_shapes=[
             pltpu.VMEM((3, 2, EXT, TILE, HALF), BF16),
             pltpu.VMEM((3, 2, HID, TILE, HALF), BF16),
@@ -432,17 +503,19 @@
             pltpu.VMEM((len(GROUPS), 2, 16, HALF), BF16),
             pltpu.VMEM((2, 2 * TILE, HALF), BF16),
             pltpu.VMEM((2, 2 * TILE, HALF), BF16),
-            pltpu.VMEM((8 * TILE + 16, HALF), F32),
             pltpu.VMEM((TILE, TILE, HALF), BF16),
             pltpu.VMEM((2, 1, HALF), F32),
             pltpu.VMEM((2, 1, HALF), F32),
+            pltpu.VMEM((1, HALF), F32),
+            pltpu.VMEM((1, HALF), F32),
             pltpu.SemaphoreType.DMA((N_SEMS,)),
             pltpu.SemaphoreType.DMA((N_SEMS,)),
-            pltpu.SemaphoreType.DMA((3,)),
+            pltpu.SemaphoreType.DMA((TILE // UNIT,)),
+            pltpu.SemaphoreType.DMA((7,)),
             pltpu.SemaphoreType.DMA((8,)),
         ],
         compiler_params=pltpu.CompilerParams(
-            collective_id=0, has_side_effects=True, vmem_limit_bytes=48 * 1024 * 1024
+            collective_id=0, has_side_effects=True, vmem_limit_bytes=64 * 1024 * 1024 - 65536
         ),
         cost_estimate=pl.CostEstimate(flops=flops, bytes_accessed=6_000_000, transcendentals=0),
     )(

time: 118 us -> 97.3 us (0.82)
  the two profiles are of different devices: /device:TPU:146 before, /device:TPU:3 now
where the time goes in v2:
time: 97.3 us; the launch traced here: 97.1 us
  Pallas kernels  95.3 us (98%)
  local copies, waits for them, and re-layouts  1.87 us (2%)
    pallas_call x1, Pallas kernels, shards(): pl.pallas_call(body, name='two_convolutions', out_shape=jax.ShapeDtypeStr...  95.3 us

profile of v2, /device:TPU:3, one launch (start us, length us, event | category | flops | bytes accessed | tf_op | source)
XLA Modules:
  0.0 97.1 jit_solution(13648529143644325708)
XLA Ops:
  0.0 95.3 %two_convolutions.1 = bf16[32,32,256]{2,1,0:T(8,128)(2,1)} custom-call(bf16[32,32,256]{2,1,0:T(8,128)(2,1)} %refs_0_.1, bf16[4608,256]{1,0:T(8,128)(2,1)} %bitcast.6, f32[1,256]{1,0:T(1,128)} %bitcast.8, f32[1,256]{1,0:T(1,128)} %bitcast.9, bf16[4608,256]{1,0:T(8,128)(2,1)} %bitcast.7, f32[1,256]{1,0:T(1,128)} %bitcast.10, f32[1,256]{1,0:T(1,128)} %bitcast.11), custom_call_target="tpu_custom_call" | custom-call | flops 7247757312 | bytes 6000000 | tf_op jit(solution)/shard_map/two_convolutions/pallas_call | solution.py:489
  95.3 1.9 %copy.9 = bf16[32,32,256]{2,1,0:T(8,128)(2,1)} copy(bf16[32,32,256]{2,1,0:T(8,128)(2,1)} %two_convolutions.1) | data formatting | bytes 1048576
